TPU v7x, 32 devices: a whole 2x2x4 slice. The times are simulated.
32 devices in a mesh: grp: 2 (over y), freq: 4 (over z), shot: 2 (over x), rcv: 2 (over core).
Axes of the slice: x: 2, y: 2, z: 4, core: 2. Of those that a mesh axis runs over, the one named last changes fastest.
Arguments:
- data: bfloat16 [2, 256, 32, 4096], P(None, 'freq', ('grp', 'shot'), 'rcv'), parts along dimension 2, may hold values from -6 to 6
- estimate: bfloat16 [2, 256, 32, 4096], P(None, 'freq', ('grp', 'shot'), 'rcv'), parts along dimension 2, may hold values from -0.09375 to 0.09375
- window_data: bfloat16 [2, 256, 32, 16], P(None, 'freq', ('grp', 'shot')), parts along dimension 2, may hold values from -6 to 6
- wavelet: float32 [2, 512], P(None, ('grp', 'freq')), parts along dimension 1, may hold values from -24 to 24
- positions: int32 [32], P(('grp', 'shot')), parts along dimension 0, may hold values from 0 to 4095
- bins: int32 [512], P('grp'), parts along dimension 0, may hold values from 0 to 399
- threshold: int32 [2], P('grp'), parts along dimension 0, may hold values from 8 to 40
- step: float32 [2], P('grp'), parts along dimension 0, may hold values from 0.25 to 1
Outputs:
- primaries: bfloat16 [1024, 32, 4096], P('freq', ('grp', 'shot'), 'rcv'), parts along dimension 1
There are 2 independent parts, one for each index of `grp`. A program takes and returns all parts, laid end to end along the dimension named above; each array names one. Nothing has to cross between parts.
All inputs are finite; a program needn't handle non-finite values.
Results may differ from a plain program's by a relative error of at most 0.0059.
The roundings to bfloat16 on the way count: a program that leaves them out, or rounds other values in their place, can miss the bound.
Values may be sent and summed in bfloat16 or wider, within the bound.
A program may use at most 64 MiB of HBM per device.

v0:
```python
from functools import partial
import math
import jax
import jax.numpy as jnp
from jax import lax
from jax.sharding import PartitionSpec as P

NF = 256
RCV = 4096
NT = 1024


def make_down(lines, spots, wavelet, offset):
    width = lines.shape[3]
    columns = offset + lax.iota(jnp.int32, width)
    select = (columns[None, None, :] == spots[None, :, None]).astype(jnp.float32)
    down_re = (wavelet[0][:, None, None] * select - lines[0].astype(jnp.float32)).astype(
        jnp.bfloat16
    )
    down_im = (wavelet[1][:, None, None] * select - lines[1].astype(jnp.float32)).astype(
        jnp.bfloat16
    )
    return (down_re, down_im)


def body(data, estimate, window_data, wavelet, positions, bins, threshold, step):
    product = partial(jnp.einsum, preferred_element_type=jnp.float32)
    offset = lax.axis_index("rcv") * data.shape[3]
    shots_all = data.shape[2] * lax.axis_size("shot")
    norm = 1.0 / math.sqrt(shots_all * RCV)
    lines, spots = (
        lax.all_gather(data, "shot", axis=2, tiled=True),
        lax.all_gather(positions, "shot", axis=0, tiled=True),
    )
    down_re, down_im = make_down(lines, spots, wavelet, offset)
    rows_re = estimate[0]
    rows_im = estimate[1]
    model_re = product("frc,fsc->frs", rows_re, down_re) - product("frc,fsc->frs", rows_im, down_im)
    model_im = product("frc,fsc->frs", rows_re, down_im) + product("frc,fsc->frs", rows_im, down_re)
    model_re, model_im = lax.psum((model_re, model_im), "rcv")
    err_re = (window_data[0].astype(jnp.float32) - model_re).astype(jnp.bfloat16)
    err_im = (window_data[1].astype(jnp.float32) - model_im).astype(jnp.bfloat16)
    grad_re = product("frs,fsc->frc", err_re, down_re) + product("frs,fsc->frc", err_im, down_im)
    grad_im = product("frs,fsc->frc", err_im, down_re) - product("frs,fsc->frc", err_re, down_im)
    step_size = step[0]
    upd_re = (estimate[0].astype(jnp.float32) - step_size * (grad_re * norm)).astype(jnp.bfloat16)
    upd_im = (estimate[1].astype(jnp.float32) - step_size * (grad_im * norm)).astype(jnp.bfloat16)
    updated = jnp.stack([upd_re, upd_im], axis=0)
    n_freq = bins.shape[0]
    times = lax.iota(jnp.int32, NT)
    phase = bins[:, None] * times[None, :] % NT
    angle = 2.0 * math.pi / NT * phase.astype(jnp.float32)
    table = jnp.concatenate([jnp.cos(angle), -jnp.sin(angle)], axis=0).astype(jnp.bfloat16)
    level = threshold[0].astype(jnp.float32) / 64.0
    amplitude = math.sqrt(RCV / NF)
    piece = lax.all_to_all(updated, "freq", split_axis=3, concat_axis=1, tiled=True)
    row_count = piece.shape[2]
    col_count = piece.shape[3]
    stacked = piece.reshape(2 * n_freq, row_count * col_count)
    trace = (
        lax.dot_general(
            table, stacked, (((0,), (0,)), ((), ())), preferred_element_type=jnp.float32
        )
        * amplitude
    )
    sparse = (jnp.sign(trace) * jnp.maximum(jnp.abs(trace) - level, 0.0)).astype(jnp.bfloat16)
    sparse = sparse.reshape(NT, row_count, col_count)
    return lax.all_to_all(sparse, "freq", split_axis=0, concat_axis=2, tiled=True)


def solution(mesh):
    return jax.shard_map(
        body,
        mesh=mesh,
        in_specs=(
            P(None, "freq", ("grp", "shot"), "rcv"),
            P(None, "freq", ("grp", "shot"), "rcv"),
            P(None, "freq", ("grp", "shot"), None),
            P(None, ("grp", "freq")),
            P(("grp", "shot")),
            P("grp"),
            P("grp"),
            P("grp"),
        ),
        out_specs=P("freq", ("grp", "shot"), "rcv"),
        check_vma=False,
    )
```

profile of v0, /device:TPU:0, one launch (start us, length us, event | category | flops | bytes accessed | tf_op | source)
XLA Modules:
  0.0 535.6 jit_solution(10995999869594317697)
XLA Ops:
  8.8 5.2 all-reduce
  14.1 101.5 %all-gather.2.cloned.1.call-done = bf16[2,64,16,2048]{3,2,1,0:T(8,128)(2,1)} async-done(((bf16[2,64,8,2048]{3,2,1,0:T(8,128)(2,1)}), bf16[2,64,16,2048]{3,2,1,0:T(8,128)(2,1)}) %all-gather.2.cloned.1.call-update) | async-done | bytes 8388624 | tf_op jit(solution)/shard_map/all_gather | solution.py:32
  115.6 5.3 fusion
  121.0 1.6 fusion.6
  122.6 1.6 fusion.4
  124.1 2.3 fusion.19
  126.4 1.9 fusion.25
  129.3 18.0 %all-reduce.4.cloned.1.call-done = (f32[64,8,16]{2,1,0:T(8,128)}, f32[64,8,16]{2,1,0:T(8,128)}) async-done(((f32[64,8,16]{2,1,0:T(8,128)}, f32[64,8,16]{2,1,0:T(8,128)}), (f32[64,8,16]{2,1,0:T(8,128)}, f32[64,8,16]{2,1,0:T(8,128)})) %all-reduce.4.cloned.1.call-update) | async-done | bytes 65552 | tf_op jit(solution)/shard_map/psum | solution.py:40
  147.3 3.1 fusion.41
  151.6 1.5 copy-done.1
  153.1 1.3 copy-done.5
  156.3 2.3 pad_maximum_fusion
  158.6 13.2 %copy.23 = bf16[2,64,8,2048]{1,2,0,3:T(8,128)(2,1)} copy(bf16[2,64,8,2048]{3,2,1,0:T(8,128)(2,1)} %pad_maximum_fusion) | data formatting | bytes 8388608 | tf_op jit(solution)/shard_map/stack | solution.py:48
  171.8 9.6 %reshape.71 = bf16[4,2,262144]{2,1,0:T(2,128)(2,1)} reshape(bf16[2048,2,8,64]{3,2,1,0:T(8,128)(2,1)} %bitcast.77) | data formatting | bytes 8388608
  181.4 5.0 all-to-all-start
  187.1 4.9 cosine_convert_fusion
  191.9 88.4 %all-to-all-done = bf16[4,2,262144]{2,1,0:T(2,128)(2,1)} async-done(((bf16[4,2,262144]{2,1,0:T(2,128)(2,1)}), bf16[4,2,262144]{2,1,0:T(2,128)(2,1)}, u32[]{:S(2)}, u32[]{:S(2)}) %all-to-all-start) | async-done | bytes 4194336 | tf_op jit(solution)/shard_map/all_to_all | solution.py:56
  280.3 9.3 %reshape.72 = bf16[2048,2,8,64]{3,2,1,0:T(8,128)(2,1)} reshape(bf16[4,2,262144]{2,1,0:T(2,128)(2,1)} %all-to-all-done) | data formatting | bytes 8388608
  289.6 12.0 %copy.24 = bf16[2,64,8,4,512]{4,2,1,3,0:T(8,128)(2,1)} copy(bf16[2,64,8,4,512]{1,2,0,4,3:T(8,128)(2,1)} %bitcast.78) | data formatting | bytes 8388608 | tf_op jit(solution)/shard_map/all_to_all | solution.py:56
  301.6 4.4 copy.28
  306.0 12.1 %multiply_convert_fusion = bf16[1024,4096]{1,0:T(8,128)(2,1)} fusion(bf16[512,4096]{1,0:T(8,128)(2,1)S(1)} %bitcast.83, f32[]{:T(128)} %bitcast.16, bf16[256,1024]{1,0:T(8,128)(2,1)S(1)} %get-tuple-element.12, bf16[256,1024]{1,0:T(8,128)(2,1)S(1)} %get-tuple-element.11), kind=kOutput, calls=%fused_computation | convolution fusion | flops 4326424576 | bytes 13631492 | tf_op jit(solution)/shard_map/dot_general | solution.py:61
  318.1 12.2 %copy.29 = bf16[128,8,8,512]{3,2,1,0:T(8,128)(2,1)} copy(bf16[128,8,8,512]{3,1,2,0:T(8,128)(2,1)} %bitcast.82) | data formatting | bytes 16777216
  330.3 190.4 %all_to_all.33 = bf16[1024,8,512]{2,1,0:T(8,128)(2,1)} all-to-all(bf16[1024,8,512]{2,1,0:T(8,128)(2,1)} %bitcast.79), channel_id=1, replica_groups=mesh['grp'=2,'freq'=4,'shot'=2,'rcv'=2] {'freq'}, dimensions={0} | all-to-all | bytes 16777216 | tf_op jit(solution)/shard_map/all_to_all | solution.py:68
  520.7 8.1 %copy.25 = bf16[4,256,8,512]{3,2,0,1:T(8,128)(2,1)} copy(bf16[4,256,8,512]{3,2,1,0:T(8,128)(2,1)} %bitcast.80) | data formatting | bytes 16777216 | tf_op jit(solution)/shard_map/all_to_all | solution.py:68
  (40 shorter events, 5.1 us)
Async XLA Ops:
  6.5 0.8 copy-start.12
  6.5 2.0 copy-start.11
  6.5 7.5 %copy-start.10 = (f32[2,64]{1,0:T(2,128)S(1)}, f32[2,64]{1,0:T(2,128)}, u32[]{:S(2)}) copy-start(f32[2,64]{1,0:T(2,128)} %param.11) | copy-start | bytes 1540
  6.5 109.1 %all-gather.2.cloned.1.call-start = ((), (), s32[]{:S(2)}) async-start(), calls=%async_computation.2 | async-start | bytes 12582912 | tf_op jit(solution)/shard_map/all_gather | solution.py:32
  7.3 140.1 %all-reduce.4.cloned.1.call-start = ((), (), s32[]{:S(2)}) async-start(), calls=%async_computation.3 | async-start | bytes 1048576 | tf_op jit(solution)/shard_map/psum | solution.py:40
  115.6 5.3 copy-start.4
  121.0 3.2 copy-start.2
  121.0 5.5 %copy-start = (bf16[64,16,2048]{2,1,0:T(8,128)(2,1)}, bf16[64,16,2048]{2,1,0:T(8,128)(2,1)S(1)}, u32[]{:S(2)}) copy-start(bf16[64,16,2048]{2,1,0:T(8,128)(2,1)S(1)} %get-tuple-element.7) | copy-start | bytes 12582916
  126.4 1.9 copy-start.8
  147.3 3.5 copy-start.3
  147.3 3.5 copy-start.7
  150.9 2.2 copy-start.1
  150.9 3.5 copy-start.5
  154.3 1.0 copy-start.6
  181.4 5.7 %copy-start.9 = (s32[256]{0:T(256)S(1)}, s32[256]{0:T(256)}, u32[]{:S(2)}) copy-start(s32[256]{0:T(256)} %param.13) | copy-start | bytes 3076
  181.4 99.0 %all-to-all-start = ((bf16[4,2,262144]{2,1,0:T(2,128)(2,1)}), bf16[4,2,262144]{2,1,0:T(2,128)(2,1)}, u32[]{:S(2)}, u32[]{:S(2)}) async-start(bf16[4,2,262144]{2,1,0:T(2,128)(2,1)} %reshape.71), calls=%async_computation | async-start | bytes 8388608 | tf_op jit(solution)/shard_map/all_to_all | solution.py:56
Sparse Core Ops, SparseCore 0:
  8.9 106.6 all-gather.1
  128.5 18.7 all-reduce.3
where the time goes:
time: 537 us; the launch traced here: 536 us
  waiting for transfers between devices  209 us (39%)
  blocking collectives  196 us (36%)
  local copies, waits for them, and re-layouts  73.1 us (14%)
  matrix products  25.2 us (5%)
  between operations  15.5 us (3%)
  other arithmetic  12.6 us (2%)
    all_to_all x1, blocking collectives, body(): lax.all_to_all(sparse, 'freq', split_axis=0, concat_axis=2, tiled=True)  190 us
    all_gather x1, waiting for transfers between devices, body(): lax.all_gather(data, 'shot', axis=2, tiled=True)  102 us
    all_to_all x1, waiting for transfers between devices, body(): lax.all_to_all(updated, 'freq', split_axis=3, concat_axis=1, tiled=True)  88.4 us
    unnamed x35, local copies, waits for them, and re-layouts  39.8 us
    psum x1, waiting for transfers between devices, body(): model_re, model_im = lax.psum((model_re, model_im), 'rcv')  18 us
    another operation x1, local copies, waits for them, and re-layouts, body(): updated = jnp.stack([upd_re, upd_im], axis=0)  13.2 us
    dot_general x1, matrix products, body(): lax.dot_general(table, stacked, (((0,), (0,)), ((), ())), preferred_eleme...  12.1 us
    all_to_all x1, local copies, waits for them, and re-layouts, body(): lax.all_to_all(updated, 'freq', split_axis=3, concat_axis=1, tiled=True)  12 us
  transfers between devices with their start and end apart: 3, of which 3 were waited for; matrix products, arithmetic and copies ran while one was open for 1% of the time, Pallas kernels for 0%

commit v1 on v0

--- a/solution.py
+++ b/solution.py
@@ -8,6 +8,18 @@
 NF = 256
 RCV = 4096
 NT = 1024
+
+
+def play_the_tiles(mine, k_dim, field_in):
+    val2 = mine.shape
+    part_now = mine.reshape(*val2[:k_dim], field_in, val2[k_dim] // field_in, *val2[k_dim + 1 :])
+    return jnp.moveaxis(part_now, k_dim, 0)
+
+
+def wait_the_columns(xin, out_dim):
+    xin = jnp.moveaxis(xin, 0, out_dim)
+    moved = xin.shape
+    return xin.reshape(*moved[:out_dim], moved[out_dim] * moved[out_dim + 1], *moved[out_dim + 2 :])
 
 
 def make_down(lines, spots, wavelet, offset):
@@ -53,7 +65,19 @@
     table = jnp.concatenate([jnp.cos(angle), -jnp.sin(angle)], axis=0).astype(jnp.bfloat16)
     level = threshold[0].astype(jnp.float32) / 64.0
     amplitude = math.sqrt(RCV / NF)
-    piece = lax.all_to_all(updated, "freq", split_axis=3, concat_axis=1, tiled=True)
+    r2 = lax.axis_size("freq")
+    state_now = lax.axis_index("freq")
+    s_next, row_out = (r2, state_now)
+    low = play_the_tiles(updated, 3, s_next)
+    tray = [low[row_out]]
+    for idx in range(1, s_next):
+        big = low[row_out ^ idx]
+        tray.append(
+            lax.ppermute(big, axis_name="freq", perm=[(i0, i0 ^ idx) for i0 in range(s_next)])
+        )
+    current_block = jnp.stack(tray, axis=0)
+    low = current_block[row_out ^ jnp.arange(s_next)]
+    piece = wait_the_columns(low, 1)
     row_count = piece.shape[2]
     col_count = piece.shape[3]
     stacked = piece.reshape(2 * n_freq, row_count * col_count)

time: 537 us -> 491 us (0.914)
  local copies, waits for them, and re-layouts: 73.1 us -> 34.5 us
  waiting for transfers between devices: 209 us -> 184 us
  blocking collectives: 196 us -> 214 us
    all_to_all x1 -> x0, waiting for transfers between devices: 88.4 us -> none  [body(): lax.all_to_all(updated, 'freq', split_axis=3, concat_axis=1, tiled=True)]
    ppermute x0 -> x3, waiting for transfers between devices: none -> 63.7 us  [body(): lax.ppermute(big, axis_name='freq', perm=[(i0, i0 ^ idx) for i0 in range(...]
    unnamed x35 -> x33, local copies, waits for them, and re-layouts: 39.8 us -> 18.8 us
    all_to_all x1, blocking collectives: 190 us -> 209 us  [body(): lax.all_to_all(sparse, 'freq', split_axis=0, concat_axis=2, tiled=True)]
    another operation x1 -> x0, local copies, waits for them, and re-layouts: 13.2 us -> none  [body(): updated = jnp.stack([upd_re, upd_im], axis=0)]
    all_to_all x1 -> x0, local copies, waits for them, and re-layouts: 12 us -> none  [body(): lax.all_to_all(updated, 'freq', split_axis=3, concat_axis=1, tiled=True)]
  transfers between devices with their start and end apart: 3 -> 5, of which waited for: 3 -> 4; matrix products, arithmetic and copies ran while one was open for 1% -> 1% of each run, Pallas kernels for 0% -> 0%
where the time goes in v1:
time: 491 us
  blocking collectives  214 us (44%)
  waiting for transfers between devices  184 us (37%)
  local copies, waits for them, and re-layouts  34.5 us (7%)
  matrix products  25.2 us (5%)
  between operations  15.6 us (3%)
  other arithmetic  12.9 us (3%)
    all_to_all x1, blocking collectives, body(): lax.all_to_all(sparse, 'freq', split_axis=0, concat_axis=2, tiled=True)  209 us
    all_gather x1, waiting for transfers between devices, body(): lax.all_gather(data, 'shot', axis=2, tiled=True)  102 us
    ppermute x3, waiting for transfers between devices, body(): lax.ppermute(big, axis_name='freq', perm=[(i0, i0 ^ idx) for i0 in range(...  63.7 us
    unnamed x33, local copies, waits for them, and re-layouts  18.8 us
    psum x1, waiting for transfers between devices, body(): model_re, model_im = lax.psum((model_re, model_im), 'rcv')  18 us
    dot_general x1, matrix products, body(): lax.dot_general(table, stacked, (((0,), (0,)), ((), ())), preferred_eleme...  12.1 us
  transfers between devices with their start and end apart: 5, of which 4 were waited for; matrix products, arithmetic and copies ran while one was open for 1% of the time, Pallas kernels for 0%

profile of v1, /device:TPU:0, one launch (start us, length us, event | category | flops | bytes accessed | tf_op | source)
XLA Modules:
  0.0 490.5 jit_solution(17897116190748681745)
XLA Ops:
  8.8 5.2 %all-reduce = s32[16]{0:T(128)S(1)} all-reduce(s32[16]{0:T(128)S(1)} %dynamic-update-slice), channel_id=1, replica_groups=mesh['grp'=2,'freq'=4,'shot'=2,'rcv'=2] {'shot'}, use_global_device_ids=true, to_apply=%add | all-reduce | flops 16 | bytes 128
  14.1 101.5 %all-gather.2.cloned.1.call-done = bf16[2,64,16,2048]{3,2,1,0:T(8,128)(2,1)} async-done(((bf16[2,64,8,2048]{3,2,1,0:T(8,128)(2,1)}), bf16[2,64,16,2048]{3,2,1,0:T(8,128)(2,1)}) %all-gather.2.cloned.1.call-update) | async-done | bytes 8388624 | tf_op jit(solution)/shard_map/all_gather | solution.py:44
  115.6 5.3 %fusion = (bf16[64,16,2048]{2,1,0:T(8,128)(2,1)S(1)}, bf16[64,16,2048]{2,1,0:T(8,128)(2,1)S(1)}) fusion(bf16[2,64,16,2048]{3,2,1,0:T(8,128)(2,1)} %all-gather.2.cloned.1.call-done, f32[64]{0:T(128)S(1)} %get-tuple-element.17, f32[16,2048]{1,0:T(8,128)S(1)} %compare_convert_fusion, f32[64]{0:T(128)S(1)} %get-tuple-element.18), kind=kLoop, calls=%fused_computation.3 | loop fusion | flops 16777216 | bytes 16908800 | tf_op jit(solution)/shard_map/convert_element_type | solution.py:32
  121.0 1.6 fusion.2
  122.6 1.6 fusion.4
  124.1 1.9 fusion.23
  126.1 2.3 fusion.17
  129.4 18.0 %all-reduce.4.cloned.1.call-done = (f32[64,8,16]{2,1,0:T(8,128)}, f32[64,8,16]{2,1,0:T(8,128)}) async-done(((f32[64,8,16]{2,1,0:T(8,128)}, f32[64,8,16]{2,1,0:T(8,128)}), (f32[64,8,16]{2,1,0:T(8,128)}, f32[64,8,16]{2,1,0:T(8,128)})) %all-reduce.4.cloned.1.call-update) | async-done | bytes 65552 | tf_op jit(solution)/shard_map/psum | solution.py:52
  147.3 3.1 fusion.50
  151.6 1.5 copy-done.1
  153.1 1.3 copy-done.5
  156.7 1.8 collective-permute-start
  158.5 2.4 collective-permute-start.1
  161.8 4.9 cosine_convert_fusion
  166.7 37.3 %collective-permute-done = bf16[2,64,8,512]{3,2,1,0:T(8,128)(2,1)S(1)} collective-permute-done((bf16[2,64,8,512]{3,2,1,0:T(8,128)(2,1)S(1)}, bf16[2,64,8,512]{3,2,1,0:T(8,128)(2,1)S(1)}, u32[]{:S(2)}, u32[]{:S(2)}) %collective-permute-start) | collective-permute-done | bytes 1048608 | tf_op jit(solution)/shard_map/ppermute | solution.py:76
  204.0 26.4 %collective-permute-done.1 = bf16[2,64,8,512]{3,2,1,0:T(8,128)(2,1)S(1)} collective-permute-done((bf16[2,64,8,512]{3,2,1,0:T(8,128)(2,1)S(1)}, bf16[2,64,8,512]{3,2,1,0:T(8,128)(2,1)S(1)}, u32[]{:S(2)}, u32[]{:S(2)}) %collective-permute-start.1) | collective-permute-done | bytes 1048608 | tf_op jit(solution)/shard_map/ppermute | solution.py:76
  230.4 2.3 pad_maximum_fusion
  232.7 4.9 %gather_fusion = bf16[4,2,64,8,512]{4,3,2,1,0:T(8,128)(2,1)} fusion(bf16[4,2,64,8,512]{4,3,2,1,0:T(8,128)(2,1)} %pad_maximum_fusion, s32[1024]{0:T(1024)S(1)} %pad_clamp_fusion), kind=kCustom, calls=%fused_computation | custom fusion | bytes 8388624 | tf_op jit(solution)/shard_map/gather | solution.py:79
  237.6 2.6 copy.17
  240.3 2.2 copy.21
  242.5 12.1 %multiply_convert_fusion = bf16[1024,4096]{1,0:T(8,128)(2,1)} fusion(bf16[512,4096]{1,0:T(8,128)(2,1)S(1)} %bitcast.92, f32[]{:T(128)} %bitcast.23, bf16[256,1024]{1,0:T(8,128)(2,1)S(1)} %get-tuple-element.16, bf16[256,1024]{1,0:T(8,128)(2,1)S(1)} %get-tuple-element.15), kind=kOutput, calls=%fused_computation.1 | convolution fusion | flops 4326424576 | bytes 13631492 | tf_op jit(solution)/shard_map/dot_general | solution.py:85
  254.6 12.2 %copy.22 = bf16[128,8,8,512]{3,2,1,0:T(8,128)(2,1)} copy(bf16[128,8,8,512]{3,1,2,0:T(8,128)(2,1)} %bitcast.91) | data formatting | bytes 16777216
  266.8 208.8 %all_to_all.18 = bf16[1024,8,512]{2,1,0:T(8,128)(2,1)} all-to-all(bf16[1024,8,512]{2,1,0:T(8,128)(2,1)} %bitcast.85), channel_id=1, replica_groups=mesh['grp'=2,'freq'=4,'shot'=2,'rcv'=2] {'freq'}, dimensions={0} | all-to-all | bytes 16777216 | tf_op jit(solution)/shard_map/all_to_all | solution.py:92
  475.6 8.1 %copy.18 = bf16[4,256,8,512]{3,2,0,1:T(8,128)(2,1)} copy(bf16[4,256,8,512]{3,2,1,0:T(8,128)(2,1)} %bitcast.86) | data formatting | bytes 16777216 | tf_op jit(solution)/shard_map/all_to_all | solution.py:92
  (45 shorter events, 5.7 us)
Async XLA Ops:
  6.5 0.8 copy-start.12
  6.5 2.0 copy-start.11
  6.5 7.5 %copy-start.10 = (f32[2,64]{1,0:T(2,128)S(1)}, f32[2,64]{1,0:T(2,128)}, u32[]{:S(2)}) copy-start(f32[2,64]{1,0:T(2,128)} %param.11) | copy-start | bytes 1540
  6.5 109.1 %all-gather.2.cloned.1.call-start = ((), (), s32[]{:S(2)}) async-start(), calls=%async_computation.1 | async-start | bytes 12582912 | tf_op jit(solution)/shard_map/all_gather | solution.py:44
  7.3 140.1 %all-reduce.4.cloned.1.call-start = ((), (), s32[]{:S(2)}) async-start(), calls=%async_computation.2 | async-start | bytes 1048576 | tf_op jit(solution)/shard_map/psum | solution.py:52
  115.6 5.3 %copy-start.4 = (bf16[2,64,8,2048]{3,2,1,0:T(8,128)(2,1)S(1)}, bf16[2,64,8,2048]{3,2,1,0:T(8,128)(2,1)}, u32[]{:S(2)}) copy-start(bf16[2,64,8,2048]{3,2,1,0:T(8,128)(2,1)} %param.9) | copy-start | bytes 12582916
  121.0 3.2 copy-start
  121.0 5.1 %copy-start.2 = (bf16[64,16,2048]{2,1,0:T(8,128)(2,1)}, bf16[64,16,2048]{2,1,0:T(8,128)(2,1)S(1)}, u32[]{:S(2)}) copy-start(bf16[64,16,2048]{2,1,0:T(8,128)(2,1)S(1)} %get-tuple-element.8) | copy-start | bytes 12582916
  126.1 2.3 copy-start.8
  147.3 3.5 copy-start.3
  147.3 3.5 copy-start.7
  150.9 2.2 copy-start.1
  150.9 3.5 copy-start.5
  154.3 1.0 copy-start.6
  156.3 5.5 %copy-start.9 = (s32[256]{0:T(256)S(1)}, s32[256]{0:T(256)}, u32[]{:S(2)}) copy-start(s32[256]{0:T(256)} %param.13) | copy-start | bytes 3076
  156.7 47.3 %collective-permute-start = (bf16[2,64,8,512]{3,2,1,0:T(8,128)(2,1)S(1)}, bf16[2,64,8,512]{3,2,1,0:T(8,128)(2,1)S(1)}, u32[]{:S(2)}, u32[]{:S(2)}) collective-permute-start(bf16[2,64,8,512]{3,2,1,0:T(8,128)(2,1)S(1)} %get-tuple-element.10), channel_id=1, source_target_pairs={{0,4},{4,0},{8,12},{12,8},{1,5},{5,1},{9,13},{13,9},{2,6},{6,2},{1... | collective-permute-start | bytes 3145736 | tf_op jit(solution)/shard_map/ppermute | solution.py:76
  158.5 71.9 %collective-permute-start.1 = (bf16[2,64,8,512]{3,2,1,0:T(8,128)(2,1)S(1)}, bf16[2,64,8,512]{3,2,1,0:T(8,128)(2,1)S(1)}, u32[]{:S(2)}, u32[]{:S(2)}) collective-permute-start(bf16[2,64,8,512]{3,2,1,0:T(8,128)(2,1)S(1)} %get-tuple-element.11), channel_id=1, source_target_pairs={{0,8},{4,12},{8,0},{12,4},{1,9},{5,13},{9,1},{13,5},{2,10},{6,14},... | collective-permute-start | bytes 3145736 | tf_op jit(solution)/shard_map/ppermute | solution.py:76
  160.9 69.5 %collective-permute-start.2 = (bf16[2,64,8,512]{3,2,1,0:T(8,128)(2,1)S(1)}, bf16[2,64,8,512]{3,2,1,0:T(8,128)(2,1)S(1)}, u32[]{:S(2)}, u32[]{:S(2)}) collective-permute-start(bf16[2,64,8,512]{3,2,1,0:T(8,128)(2,1)S(1)} %get-tuple-element.12), channel_id=1, source_target_pairs={{0,12},{4,8},{8,4},{12,0},{1,13},{5,9},{9,5},{13,1},{2,14},{6,10},... | collective-permute-start | bytes 3145736 | tf_op jit(solution)/shard_map/ppermute | solution.py:76
Sparse Core Ops, SparseCore 0:
  8.9 106.6 all-gather.1
  128.5 18.7 all-reduce.3
